TPU v7x, 256 devices: a whole 4x4x8 slice. The times are simulated.
256 devices in a mesh: px: 32 (over x, y, core), py: 8 (over z).
Axes of the slice: x: 4, y: 4, z: 8, core: 2. Of those that a mesh axis runs over, the one named last changes fastest.
Arguments:
- forcing: float32 [3, 224, 56, 7, 128], P(None, 'px', 'py'), may hold values from -600 to 600
- initial_guess: float32 [3, 224, 56, 7, 128], P(None, 'px', 'py'), may hold values from -3 to 3
- forward_velocity: bfloat16 [3, 224, 56, 7, 128], P(None, 'px', 'py'), may hold values from -4 to 4
- free_mask: int32 [224, 56, 7, 128], P('px', 'py'), may hold values 0 or 1
Outputs:
- adjoint_velocity: float32 [3, 224, 56, 7, 128], P(None, 'px', 'py')
- search_direction: float32 [3, 224, 56, 7, 128], P(None, 'px', 'py')
Inputs may be any that keep to these rules, and one draw needn't show every extreme that they name: `free_mask`: 1 marks a free node, 0 a node held at its initial guess.
All inputs are finite; a program needn't handle non-finite values. No bound on the sum of `free_mask` on one device may be relied on, other than what follows from the above.
Results may differ from a plain program's by a relative error of at most 0.00085.
Values sent between devices are 32-bit elements; how exact they have to be, the bound alone decides.
A program may use at most 64 MiB of HBM per device.

v0:
```python
import jax
import jax.numpy as jnp
import numpy as np
from jax import lax
from jax.sharding import PartitionSpec as P

ITERS = 2


VISC_BASE = 0.5
VISC_GAIN = 0.5
HELMHOLTZ = 20.0


def shifted(value, axis, by):
    count = lax.axis_size(axis)
    return lax.ppermute(value, axis, [(i, (i + by) % count) for i in range(count)])


def passed_along(block, axis, distance):
    devices = range(lax.axis_size(axis))
    route = [(i - distance, i) for i in devices if i - distance in devices]
    return lax.ppermute(block, axis, route)


def gll_tables():
    poly_order = 7
    gll_points = np.array(
        [
            -1.0,
            -0.8717401485096066,
            -0.5917001814331423,
            -0.20929921790247888,
            0.20929921790247888,
            0.5917001814331423,
            0.8717401485096066,
            1.0,
        ]
    )
    previous = np.ones(8)
    legendre = gll_points.copy()
    for degree in range(1, poly_order):
        following = ((2 * degree + 1) * gll_points * legendre - degree * previous) / (degree + 1)
        previous = legendre
        legendre = following
    quad_weights = 2.0 / (poly_order * (poly_order + 1) * legendre**2)
    derivative = np.zeros((8, 8))
    for target in range(8):
        for source in range(8):
            if target != source:
                derivative[target, source] = (
                    legendre[target] / legendre[source] / (gll_points[target] - gll_points[source])
                )
    derivative[0, 0] = -poly_order * (poly_order + 1) / 4.0
    derivative[7, 7] = poly_order * (poly_order + 1) / 4.0
    node_weights = quad_weights[:7].copy()
    node_weights[0] = 2.0 * quad_weights[0]
    return (quad_weights, derivative, node_weights)


def line_weights(length):
    node_weights = gll_tables()[2]
    return jnp.asarray(np.tile(node_weights, length // 7), jnp.float32)


def local_view(values, dimension, elements):
    leading = lax.slice_in_dim(values, 0, 7 * elements, axis=dimension)
    leading = leading.reshape(
        values.shape[:dimension] + (elements, 7) + values.shape[dimension + 1 :]
    )
    closing = lax.slice_in_dim(values, 7, 7 * elements + 1, stride=7, axis=dimension)
    closing = jnp.expand_dims(closing, dimension + 1)
    return jnp.concatenate([leading, closing], axis=dimension + 1)


def fold_view(local_part, dimension, elements):
    leading = lax.slice_in_dim(local_part, 0, 7, axis=dimension + 1)
    out_shape = local_part.shape[:dimension] + (7 * elements,) + local_part.shape[dimension + 2 :]
    leading = leading.reshape(out_shape)
    closing = lax.slice_in_dim(local_part, 7, 8, axis=dimension + 1)
    padding = jnp.zeros(
        closing.shape[: dimension + 1] + (6,) + closing.shape[dimension + 2 :], local_part.dtype
    )
    closing = jnp.concatenate([padding, closing], axis=dimension + 1).reshape(out_shape)
    zero_node = jnp.zeros(
        out_shape[:dimension] + (1,) + out_shape[dimension + 1 :], local_part.dtype
    )
    return jnp.concatenate([leading, zero_node], axis=dimension) + jnp.concatenate(
        [zero_node, closing], axis=dimension
    )


def z_view(values):
    first_layer = values[..., 0:1, :]
    return jnp.concatenate([values, jnp.roll(first_layer, -1, axis=-1)], axis=-2)


def z_fold(local_part):
    first_node = local_part[..., 0:1, :] + jnp.roll(local_part[..., 7:8, :], 1, axis=-1)
    return jnp.concatenate([first_node, local_part[..., 1:7, :]], axis=-2)


def kernel(values, coef_part, trailing):
    quad_weights, derivative, node_weights = gll_tables()
    deriv_table = jnp.asarray(derivative, jnp.float32)
    weight_column = jnp.asarray(quad_weights, jnp.float32).reshape((8,) + (1,) * trailing)
    index_tail = "sab"[3 - trailing :]
    gradient = jnp.einsum(
        "mk,...k" + index_tail + "->...m" + index_tail,
        deriv_table,
        values,
        precision=lax.Precision.HIGHEST,
    )
    flux_term = gradient * (weight_column * coef_part)
    return jnp.einsum(
        "mk,...m" + index_tail + "->...k" + index_tail,
        deriv_table,
        flux_term,
        precision=lax.Precision.HIGHEST,
    )


def diag_kernel(coef_part, trailing):
    quad_weights, derivative, node_weights = gll_tables()
    square_table = jnp.asarray(derivative * derivative, jnp.float32)
    weight_column = jnp.asarray(quad_weights, jnp.float32).reshape((8,) + (1,) * trailing)
    index_tail = "sab"[3 - trailing :]
    return jnp.einsum(
        "mk,...m" + index_tail + "->...k" + index_tail,
        square_table,
        weight_column * coef_part,
        precision=lax.Precision.HIGHEST,
    )


def element_factor():
    return 1.0


def direction_term(values, coef_ext, from_right):
    field_dim = values.ndim - from_right
    coef_dim = coef_ext.ndim - from_right
    elements = (values.shape[field_dim] - 1) // 7
    local_part = kernel(
        local_view(values, field_dim, elements),
        local_view(coef_ext, coef_dim, elements),
        from_right - 1,
    )
    local_part = local_part * element_factor()
    return fold_view(local_part, field_dim, elements)


def diag_term(coef_ext, from_right):
    coef_dim = coef_ext.ndim - from_right
    elements = (coef_ext.shape[coef_dim] - 1) // 7
    local_part = diag_kernel(local_view(coef_ext, coef_dim, elements), from_right - 1)
    local_part = local_part * element_factor()
    return fold_view(local_part, coef_dim, elements)


def extend_x(values):
    dimension = values.ndim - 4
    first_layer = lax.slice_in_dim(values, 0, 1, axis=dimension)
    upper_part = shifted(first_layer, "px", -1)
    return jnp.concatenate([values, upper_part], axis=dimension)


def extend_y(values):
    dimension = values.ndim - 3
    first_layer = lax.slice_in_dim(values, 0, 1, axis=dimension)
    upper_part = passed_along(first_layer, "py", -1)
    return jnp.concatenate([values, upper_part], axis=dimension)


def reduce_x(values):
    dimension = values.ndim - 4
    length = values.shape[dimension]
    last_node = lax.slice_in_dim(values, length - 1, length, axis=dimension)
    arrived = shifted(last_node, "px", 1)
    first_node = lax.slice_in_dim(values, 0, 1, axis=dimension) + arrived
    return jnp.concatenate(
        [first_node, lax.slice_in_dim(values, 1, length - 1, axis=dimension)], axis=dimension
    )


def reduce_y(values):
    dimension = values.ndim - 3
    length = values.shape[dimension]
    last_node = lax.slice_in_dim(values, length - 1, length, axis=dimension)
    arrived = passed_along(last_node, "py", 1)
    first_node = lax.slice_in_dim(values, 0, 1, axis=dimension) + arrived
    return jnp.concatenate(
        [first_node, lax.slice_in_dim(values, 1, length - 1, axis=dimension)], axis=dimension
    )


def spread(totals):
    return totals.reshape(3, 1, 1, 1, 1)


def energy_sum(residual, precond):
    return lax.psum(jnp.sum(residual * precond, axis=(1, 2, 3, 4)), ("px", "py"))


def body(forcing, initial_guess, forward_velocity, free_mask):
    free_float = free_mask.astype(jnp.float32)
    speed_sq = jnp.sum(jnp.square(forward_velocity.astype(jnp.float32)), axis=0)
    viscosity = VISC_BASE + VISC_GAIN * speed_sq
    weight_x = line_weights(free_mask.shape[0])[:, None, None, None]
    weight_y = line_weights(free_mask.shape[1])[:, None, None]
    weight_z = line_weights(7)[:, None]
    coef_x = viscosity * weight_y * weight_z
    coef_y = viscosity * weight_x * weight_z
    coef_z = viscosity * weight_x * weight_y
    mass_diag = weight_x * weight_y * weight_z * jnp.ones((free_mask.shape[3],), jnp.float32)
    coef_x_ext = extend_x(coef_x)
    coef_y_ext = extend_y(coef_y)
    diag_x = reduce_x(diag_term(coef_x_ext, 4))
    diag_y = reduce_y(diag_term(coef_y_ext, 3))
    diag_z = z_fold(diag_kernel(z_view(coef_z), 1))
    diagonal = diag_x + diag_y + diag_z + HELMHOLTZ * mass_diag
    coef_z_view = z_view(coef_z)

    def operate(values):
        term_x = reduce_x(direction_term(extend_x(values), coef_x_ext, 4))
        term_y = reduce_y(direction_term(extend_y(values), coef_y_ext, 3))
        term_z = z_fold(kernel(z_view(values), coef_z_view, 1))
        return free_float * (term_x + term_y + term_z + HELMHOLTZ * mass_diag * values)

    right_side = free_float * mass_diag * forcing
    solution = initial_guess
    residual = right_side - operate(initial_guess)
    precond = residual / diagonal
    energy_now = energy_sum(residual, precond)
    direction = precond
    for iteration in range(ITERS):
        applied = operate(direction)
        curvature = lax.psum(jnp.sum(direction * applied, axis=(1, 2, 3, 4)), ("px", "py"))
        step_length = spread(energy_now / curvature)
        solution = solution + step_length * direction
        residual = residual - step_length * applied
        precond = residual / diagonal
        energy_next = energy_sum(residual, precond)
        direction = precond + spread(energy_next / energy_now) * direction
        energy_now = energy_next
    return (solution, direction)


def solution(mesh):
    placed = (
        P(None, "px", "py", None, None),
        P(None, "px", "py", None, None),
        P(None, "px", "py", None, None),
        P("px", "py", None, None),
    )
    return jax.shard_map(
        body,
        mesh=mesh,
        in_specs=placed,
        out_specs=(P(None, "px", "py", None, None), P(None, "px", "py", None, None)),
        check_vma=False,
    )
```

profile of v0, /device:TPU:1, one launch (start us, length us, event | category | flops | bytes accessed | tf_op | source)
XLA Modules:
  0.0 393.7 jit_solution(17573299616021403080)
XLA Ops:
  0.6 1.1 multiply_reduce_fusion.5
  1.9 1.3 collective-permute-start.4
  3.8 3.2 collective-permute-start.1
  7.7 2.9 collective-permute-start
  11.3 1.3 collective-permute-start.3
  19.0 0.9 maximum_multiply_fusion
  20.3 4.8 %collective-permute-start.7 = (f32[7,1,7,128]{3,0,2,1:T(8,128)S(1)}, f32[7,1,7,128]{3,0,2,1:T(8,128)S(1)}, u32[]{:S(2)}, u32[]{:S(2)}) collective-permute-start(f32[7,1,7,128]{3,0,2,1:T(8,128)S(1)} %pad_add_fusion.14), channel_id=1, source_target_pairs={{0,1},{1,2},{2,3},{3,4},{4,5},{5,6},{6,7},{8,9},{9,10},{10,11},{11... | collective-permute-start | bytes 75272 | tf_op jit(solution)/shard_map/ppermute | solution.py:23
  25.2 0.8 maximum_multiply_fusion.2
  26.6 1.8 collective-permute-done.6
  28.6 1.6 fusion.4
  31.2 1.5 collective-permute-start.2
  34.5 3.7 collective-permute-start.5
  38.6 1.0 collective-permute-done.5
  42.1 6.1 %collective-permute-start.8 = (f32[3,1,7,7,128]{4,1,3,2,0:T(1,128)S(1)}, f32[3,1,7,7,128]{4,1,3,2,0:T(1,128)S(1)}, u32[]{:S(2)}, u32[]{:S(2)}) collective-permute-start(f32[3,1,7,7,128]{4,1,3,2,0:T(1,128)S(1)} %slice.347), channel_id=1, source_target_pairs={{0,248},{8,0},{16,8},{24,16},{32,24},{40,32},{48,40},{56,48},{64,5... | collective-permute-start | bytes 225800 | tf_op jit(solution)/shard_map/ppermute | solution.py:17
  48.2 1.3 collective-permute-start.10
  51.6 2.1 collective-permute-done.10
  55.5 4.1 %collective-permute-start.11 = (f32[3,7,1,7,128]{4,1,3,2,0:T(8,128)S(1)}, f32[3,7,1,7,128]{4,1,3,2,0:T(8,128)S(1)}, u32[]{:S(2)}, u32[]{:S(2)}) collective-permute-start(f32[3,7,1,7,128]{4,1,3,2,0:T(8,128)S(1)} %pad_add_fusion.9), channel_id=1, source_target_pairs={{0,1},{1,2},{2,3},{3,4},{4,5},{5,6},{6,7},{8,9},{9,10},{10,11},{11... | collective-permute-start | bytes 225800 | tf_op jit(solution)/shard_map/ppermute | solution.py:23
  59.7 1.0 collective-permute-done.9
  61.7 84.8 %all-reduce.24 = (f32[3]{0:T(128)S(1)}, f32[3]{0:T(128)S(1)}) all-reduce(f32[3]{0:T(128)S(1)} %get-tuple-element.11, f32[3]{0:T(128)S(1)} %get-tuple-element.10), channel_id=1, replica_groups=mesh['px'=32,'py'=8] {'px','py'}, use_global_device_ids=true, to_apply=%region_2.3 | all-reduce | flops 6 | bytes 48 | tf_op jit(solution)/shard_map/psum | solution.py:202
  146.8 74.6 %psum.37 = f32[3]{0:T(128)S(1)} all-reduce(f32[3]{0:T(128)S(1)} %get-tuple-element.16), channel_id=1, replica_groups=mesh['px'=32,'py'=8] {'px','py'}, use_global_device_ids=true, to_apply=%region_6.7 | all-reduce | flops 3 | bytes 24 | tf_op jit(solution)/shard_map/psum | solution.py:202
  221.9 0.8 copy-done.2
  224.3 0.8 collective-permute-start.12
  225.0 1.3 collective-permute-start.14
  226.5 1.7 collective-permute-done.12
  230.3 0.9 copy-done.4
  232.7 2.3 collective-permute-start.13
  235.1 1.8 collective-permute-start.15
  237.2 1.7 collective-permute-done.15
  239.4 78.2 %psum.38 = f32[3]{0:T(128)S(1)} all-reduce(f32[3]{0:T(128)S(1)} %get-tuple-element.14), channel_id=1, replica_groups=mesh['px'=32,'py'=8] {'px','py'}, use_global_device_ids=true, to_apply=%region_8.9 | all-reduce | flops 3 | bytes 24 | tf_op jit(solution)/shard_map/psum | solution.py:238
  317.9 73.5 %psum.39 = f32[3]{0:T(128)S(1)} all-reduce(f32[3]{0:T(128)S(1)} %multiply_reduce_fusion), channel_id=1, replica_groups=mesh['px'=32,'py'=8] {'px','py'}, use_global_device_ids=true, to_apply=%region_10.11 | all-reduce | flops 3 | bytes 24 | tf_op jit(solution)/shard_map/psum | solution.py:202
  391.8 0.9 copy.203
  392.8 0.9 copy.204
  (177 shorter events, 27.4 us)
Async XLA Ops:
  0.6 1.1 copy-start.11
  1.9 17.1 %collective-permute-start.4 = (f32[7,1,7,128]{3,0,2,1:T(8,128)S(1)}, f32[7,1,7,128]{3,0,2,1:T(8,128)}, u32[]{:S(2)}, u32[]{:S(2)}) collective-permute-start(f32[7,1,7,128]{3,0,2,1:T(8,128)S(1)} %slice.328), channel_id=1, source_target_pairs={{1,0},{2,1},{3,2},{4,3},{5,4},{6,5},{7,6},{9,8},{10,9},{11,10},{12... | collective-permute-start | bytes 75272 | tf_op jit(solution)/shard_map/ppermute | solution.py:23
  3.8 3.2 slice-start
  3.8 21.4 %collective-permute-start.1 = (f32[1,7,7,128]{3,0,2,1:T(1,128)}, f32[1,7,7,128]{3,0,2,1:T(1,128)}, u32[]{:S(2)}, u32[]{:S(2)}) collective-permute-start(f32[1,7,7,128]{3,0,2,1:T(1,128)} %slice.324), channel_id=1, source_target_pairs={{0,248},{8,0},{16,8},{24,16},{32,24},{40,32},{48,40},{56,48},{64,5... | collective-permute-start | bytes 75272 | tf_op jit(solution)/shard_map/ppermute | solution.py:17
  7.7 2.9 slice-start.1
  7.7 20.9 %collective-permute-start = (f32[3,1,7,7,128]{4,1,3,2,0:T(1,128)}, f32[3,1,7,7,128]{4,1,3,2,0:T(1,128)}, u32[]{:S(2)}, u32[]{:S(2)}) collective-permute-start(f32[3,1,7,7,128]{4,1,3,2,0:T(1,128)} %copy.257), channel_id=1, source_target_pairs={{0,248},{8,0},{16,8},{24,16},{32,24},{40,32},{48,40},{56,48},{64,5... | collective-permute-start | bytes 225800 | tf_op jit(solution)/shard_map/ppermute | solution.py:17
  11.3 21.5 %collective-permute-start.3 = (f32[3,7,1,7,128]{4,2,3,1,0:T(1,128)}, f32[3,7,1,7,128]{4,2,3,1,0:T(1,128)S(1)}, u32[]{:S(2)}, u32[]{:S(2)}) collective-permute-start(f32[3,7,1,7,128]{4,2,3,1,0:T(1,128)} %copy.258), channel_id=1, source_target_pairs={{1,0},{2,1},{3,2},{4,3},{5,4},{6,5},{7,6},{9,8},{10,9},{11,10},{12... | collective-permute-start | bytes 225800 | tf_op jit(solution)/shard_map/ppermute | solution.py:23
  12.7 0.7 copy-start.12
  13.4 0.7 copy-start.10
  13.5 1.1 copy-start
  14.0 26.4 %copy-start.1 = (f32[7,7,8,128]{3,2,1,0:T(8,128)}, f32[7,7,8,128]{3,2,1,0:T(8,128)S(1)}, u32[]{:S(2)}) copy-start(f32[7,7,8,128]{3,2,1,0:T(8,128)S(1)} %copy.176) | copy-start | bytes 602116
  15.0 0.7 copy-start.7
  17.4 0.9 copy-start.8
  18.9 42.2 %copy-start.5 = (f32[7,7,7,128]{3,0,2,1:T(8,128)}, f32[7,7,7,128]{3,0,2,1:T(8,128)S(1)}, u32[]{:S(2)}) copy-start(f32[7,7,7,128]{3,0,2,1:T(8,128)S(1)} %copy.162) | copy-start | bytes 526852
  19.9 33.9 %copy-start.3 = (f32[7,8,7,128]{3,1,2,0:T(8,128)}, f32[7,8,7,128]{3,1,2,0:T(8,128)S(1)}, u32[]{:S(2)}) copy-start(f32[7,8,7,128]{3,1,2,0:T(8,128)S(1)} %copy.170) | copy-start | bytes 602116
  20.3 6.2 %collective-permute-start.7 = (f32[7,1,7,128]{3,0,2,1:T(8,128)S(1)}, f32[7,1,7,128]{3,0,2,1:T(8,128)S(1)}, u32[]{:S(2)}, u32[]{:S(2)}) collective-permute-start(f32[7,1,7,128]{3,0,2,1:T(8,128)S(1)} %pad_add_fusion.14), channel_id=1, source_target_pairs={{0,1},{1,2},{2,3},{3,4},{4,5},{5,6},{6,7},{8,9},{9,10},{10,11},{11... | collective-permute-start | bytes 75272 | tf_op jit(solution)/shard_map/ppermute | solution.py:23
  26.5 1.9 collective-permute-start.6
  31.2 7.1 %collective-permute-start.2 = (f32[3,1,7,7,128]{4,1,3,2,0:T(1,128)S(1)}, f32[3,1,7,7,128]{4,1,3,2,0:T(1,128)S(1)}, u32[]{:S(2)}, u32[]{:S(2)}) collective-permute-start(f32[3,1,7,7,128]{4,1,3,2,0:T(1,128)S(1)} %pad_add_fusion.13), channel_id=1, source_target_pairs={{0,8},{8,16},{16,24},{24,32},{32,40},{40,48},{48,56},{56,64},{64,7... | collective-permute-start | bytes 225800 | tf_op jit(solution)/shard_map/ppermute | solution.py:17
  34.5 5.1 %collective-permute-start.5 = (f32[3,7,1,7,128]{4,1,3,2,0:T(8,128)S(1)}, f32[3,7,1,7,128]{4,1,3,2,0:T(8,128)S(1)}, u32[]{:S(2)}, u32[]{:S(2)}) collective-permute-start(f32[3,7,1,7,128]{4,1,3,2,0:T(8,128)S(1)} %pad_add_fusion.10), channel_id=1, source_target_pairs={{0,1},{1,2},{2,3},{3,4},{4,5},{5,6},{6,7},{8,9},{9,10},{10,11},{11... | collective-permute-start | bytes 225800 | tf_op jit(solution)/shard_map/ppermute | solution.py:23
  38.5 1.1 copy-start.9
  42.1 7.5 %collective-permute-start.8 = (f32[3,1,7,7,128]{4,1,3,2,0:T(1,128)S(1)}, f32[3,1,7,7,128]{4,1,3,2,0:T(1,128)S(1)}, u32[]{:S(2)}, u32[]{:S(2)}) collective-permute-start(f32[3,1,7,7,128]{4,1,3,2,0:T(1,128)S(1)} %slice.347), channel_id=1, source_target_pairs={{0,248},{8,0},{16,8},{24,16},{32,24},{40,32},{48,40},{56,48},{64,5... | collective-permute-start | bytes 225800 | tf_op jit(solution)/shard_map/ppermute | solution.py:17
  48.2 5.5 %collective-permute-start.10 = (f32[3,7,1,7,128]{4,1,3,2,0:T(8,128)S(1)}, f32[3,7,1,7,128]{4,1,3,2,0:T(8,128)S(1)}, u32[]{:S(2)}, u32[]{:S(2)}) collective-permute-start(f32[3,7,1,7,128]{4,1,3,2,0:T(8,128)S(1)} %slice.350), channel_id=1, source_target_pairs={{1,0},{2,1},{3,2},{4,3},{5,4},{6,5},{7,6},{9,8},{10,9},{11,10},{12... | collective-permute-start | bytes 225800 | tf_op jit(solution)/shard_map/ppermute | solution.py:23
  55.3 5.4 %collective-permute-start.9 = (f32[3,1,7,7,128]{4,1,3,2,0:T(1,128)S(1)}, f32[3,1,7,7,128]{4,1,3,2,0:T(1,128)S(1)}, u32[]{:S(2)}, u32[]{:S(2)}) collective-permute-start(f32[3,1,7,7,128]{4,1,3,2,0:T(1,128)S(1)} %pad_add_fusion.12), channel_id=1, source_target_pairs={{0,8},{8,16},{16,24},{24,32},{32,40},{40,48},{48,56},{56,64},{64,7... | collective-permute-start | bytes 225800 | tf_op jit(solution)/shard_map/ppermute | solution.py:17
  55.5 5.6 %collective-permute-start.11 = (f32[3,7,1,7,128]{4,1,3,2,0:T(8,128)S(1)}, f32[3,7,1,7,128]{4,1,3,2,0:T(8,128)S(1)}, u32[]{:S(2)}, u32[]{:S(2)}) collective-permute-start(f32[3,7,1,7,128]{4,1,3,2,0:T(8,128)S(1)} %pad_add_fusion.9), channel_id=1, source_target_pairs={{0,1},{1,2},{2,3},{3,4},{4,5},{5,6},{6,7},{8,9},{9,10},{10,11},{11... | collective-permute-start | bytes 225800 | tf_op jit(solution)/shard_map/ppermute | solution.py:23
  221.7 0.9 copy-start.2
  224.3 3.9 collective-permute-start.12
  225.0 5.2 %collective-permute-start.14 = (f32[3,7,1,7,128]{4,1,3,2,0:T(8,128)S(1)}, f32[3,7,1,7,128]{4,1,3,2,0:T(8,128)S(1)}, u32[]{:S(2)}, u32[]{:S(2)}) collective-permute-start(f32[3,7,1,7,128]{4,1,3,2,0:T(8,128)S(1)} %slice.362), channel_id=1, source_target_pairs={{1,0},{2,1},{3,2},{4,3},{5,4},{6,5},{7,6},{9,8},{10,9},{11,10},{12... | collective-permute-start | bytes 225800 | tf_op jit(solution)/shard_map/ppermute | solution.py:23
  230.2 0.9 copy-start.4
  232.7 4.3 %collective-permute-start.13 = (f32[3,1,7,7,128]{4,1,3,2,0:T(1,128)S(1)}, f32[3,1,7,7,128]{4,1,3,2,0:T(1,128)S(1)}, u32[]{:S(2)}, u32[]{:S(2)}) collective-permute-start(f32[3,1,7,7,128]{4,1,3,2,0:T(1,128)S(1)} %pad_add_fusion.11), channel_id=1, source_target_pairs={{0,8},{8,16},{16,24},{24,32},{32,40},{40,48},{48,56},{56,64},{64,7... | collective-permute-start | bytes 225800 | tf_op jit(solution)/shard_map/ppermute | solution.py:17
  235.1 3.8 collective-permute-start.15
  237.2 1.7 copy-start.6
where the time goes:
time: 395 us; the launch traced here: 394 us
  blocking collectives  311 us (79%)
  starting transfers between devices  36.5 us (9%)
  matrix products  14.2 us (4%)
  local copies, waits for them, and re-layouts  11.6 us (3%)
  waiting for transfers between devices  9.8 us (2%)
  other arithmetic  8.82 us (2%)
    psum x3, blocking collectives, energy_sum(): lax.psum(jnp.sum(residual * precond, axis=(1, 2, 3, 4)), ('px', 'py'))  233 us
    psum x1, blocking collectives, body(): lax.psum(jnp.sum(direction * applied, axis=(1, 2, 3, 4)), ('px', 'py'))  78.2 us
    ppermute x8, starting transfers between devices, passed_along(): return lax.ppermute(block, axis, route)  19.6 us
    ppermute x8, starting transfers between devices, shifted(): lax.ppermute(value, axis, [(i, (i + by) % count) for i in range(count)])  16.9 us
  transfers between devices with their start and end apart: 16, of which 8 were waited for; matrix products, arithmetic and copies ran while one was open for 5% of the time, Pallas kernels for 0%

commit v1 on v0

v1 whole, which is shorter than its diff:
```python
import functools

import jax
import jax.numpy as jnp
import numpy as np
from jax import lax
from jax.experimental import pallas as pl
from jax.experimental.pallas import tpu as pltpu
from jax.sharding import PartitionSpec as P

MESH = pl.DeviceIdType.MESH
HELMHOLTZ = 20.0


def gll_tables():
    poly_order = 7
    gll_points = np.array(
        [
            -1.0,
            -0.8717401485096066,
            -0.5917001814331423,
            -0.20929921790247888,
            0.20929921790247888,
            0.5917001814331423,
            0.8717401485096066,
            1.0,
        ]
    )
    previous = np.ones(8)
    legendre = gll_points.copy()
    for degree in range(1, poly_order):
        following = ((2 * degree + 1) * gll_points * legendre - degree * previous) / (degree + 1)
        previous = legendre
        legendre = following
    quad_weights = 2.0 / (poly_order * (poly_order + 1) * legendre**2)
    derivative = np.zeros((8, 8))
    for target in range(8):
        for source in range(8):
            if target != source:
                derivative[target, source] = (
                    legendre[target] / legendre[source] / (gll_points[target] - gll_points[source])
                )
    derivative[0, 0] = -poly_order * (poly_order + 1) / 4.0
    derivative[7, 7] = poly_order * (poly_order + 1) / 4.0
    node_weights = quad_weights[:7].copy()
    node_weights[0] = 2.0 * quad_weights[0]
    return quad_weights, derivative, node_weights


QW, DM, NW = gll_tables()
EVEN = [[float(DM[m, k] + DM[m, 7 - k]) / 2 for k in range(4)] for m in range(4)]
ODD = [[float(DM[m, k] - DM[m, 7 - k]) / 2 for k in range(4)] for m in range(4)]
D77 = float(DM[7, 7])

NZ = 5


def z_constants():
    table = np.zeros((NZ * 8 + 2, 8, 128), np.float32)
    for s in range(NZ):
        for t in range(8):
            for a in range(8):
                m = (a + t) % 8
                table[s * 8 + t, a, :] = DM[m, a] * DM[m, (a + s) % 8]
    for a in range(8):
        table[NZ * 8, a, :] = QW[a]
        table[NZ * 8 + 1, a, :] = NW[a] if a < 7 else 0.0
    return table


def total(terms):
    terms = list(terms)
    while len(terms) > 1:
        terms = [
            terms[i] + terms[i + 1] if i + 1 < len(terms) else terms[i]
            for i in range(0, len(terms), 2)
        ]
    return terms[0]


def by_index(i, table):
    inner = jnp.where((i == 2) | (i == 5), float(table[2]), float(table[3]))
    inner = jnp.where((i == 1) | (i == 6), float(table[1]), inner)
    return jnp.where(i == 0, float(table[0]), inner)


def line_apply(v, kappa):
    p = [v[0]] + [v[j] + v[7 - j] for j in range(1, 4)]
    q = [v[0]] + [v[j] - v[7 - j] for j in range(1, 4)]
    a, b = [], []
    for m in range(4):
        even = total(EVEN[m][k] * p[k] for k in range(4))
        odd = total(ODD[m][k] * q[k] for k in range(4))
        first = kappa[m] * (odd + even)
        last = kappa[7 - m] * (odd - even)
        a.append(first - last)
        b.append(first + last)
    out = [None] * 8
    for k in range(4):
        r = total(EVEN[m][k] * a[m] for m in range(4))
        t = total(ODD[m][k] * b[m] for m in range(4))
        out[k] = r + t
        if k:
            out[7 - k] = r - t
    return out[:7]


def close_rows(tile, last_row):
    moved = pltpu.roll(pltpu.roll(tile, 127, 1), 7, 0)
    return jnp.where(last_row, moved, tile)


def fold_rows(tile, first_row):
    moved = pltpu.roll(pltpu.roll(tile, 1, 1), 1, 0)
    return jnp.where(first_row, tile + moved, tile)


def turned(tile, s):
    return pltpu.roll(tile, 8 - s, 0) if s else tile


def z_apply(closed, diagonals, first_row):
    terms = [diagonals[0] * closed, diagonals[4] * turned(closed, 4)]
    for s in range(1, 4):
        terms.append(diagonals[s] * turned(closed, s))
        terms.append(pltpu.roll(diagonals[s] * closed, s, 0))
    return fold_rows(total(terms), first_row)


def group(px, py, phase):
    x, y, c = px // 8, lax.rem(px // 2, 4), lax.rem(px, 2)
    if phase == 0:
        offsets = [(0, 0, 0, d) for d in (4, 3, 5, 2, 6, 1, 7)]
    else:
        offsets = [
            (dx, dy, dc, 0)
            for dx in (2, 1, 3, 0)
            for dy in (2, 1, 3, 0)
            for dc in (1, 0)
            if dx or dy or dc
        ]
    out = []
    for dx, dy, dc, dz in offsets:
        nx, ny, nc = lax.rem(x + dx, 4), lax.rem(y + dy, 4), lax.rem(c + dc, 2)
        out.append((nx * 8 + ny * 2 + nc, lax.rem(py + dz, 8)))
    return out


GROUPS = (7, 31)


def main_kernel(
    f_hbm, x_hbm, fv_hbm, m_hbm, z_hbm,
    v1, v2, v3, coef,
    f7, x7, fv7, m7, zc, v0, fm, cv, acc, kx, ky, bx, by, zd, mdi, dg,
    s_out, rv, rs, rb, row_out, rows_in,
    load_sem, send_sem, recv_sem, set_send, set_recv, row_send, row_recv,
):
    px = lax.axis_index("px")
    py = lax.axis_index("py")
    not_first = py > 0
    not_last = py < 7
    prev_x, next_x = (lax.rem(px + 31, 32), py), (lax.rem(px + 1, 32), py)
    prev_y, next_y = (px, lax.rem(py + 7, 8)), (px, lax.rem(py + 1, 8))

    loads = [
        pltpu.make_async_copy(src, dst, load_sem.at[i])
        for i, (src, dst) in enumerate(
            ((fv_hbm, fv7), (x_hbm, x7), (f_hbm, f7), (z_hbm, zc), (m_hbm, m7))
        )
    ]
    for load in loads:
        load.start()

    partners = [group(px, py, phase) for phase in (0, 1)]
    barrier = pltpu.get_barrier_semaphore()
    for device in partners[1] + partners[0]:
        pl.semaphore_signal(barrier, inc=1, device_id=device, device_id_type=MESH)

    zero_row = jnp.zeros((1, 128), jnp.float32)
    zero_face = jnp.zeros((7, 8, 128), jnp.float32)

    @pl.when(py == 0)
    def _():
        rb[1] = zero_face
        for r in range(3):
            for c in range(3):
                rs[r, c, 1, 0] = zero_face
                rs[r, c, 1, 1] = zero_face

    @pl.when(py == 7)
    def _():
        ky[:, 7] = zero_face
        for r in range(3):
            for c in range(3):
                rv[r, c, 1] = zero_face

    rows = lax.broadcasted_iota(jnp.int32, (8, 128), 0)
    lanes = lax.broadcasted_iota(jnp.int32, (8, 128), 1)
    first_row, last_row = rows == 0, rows == 7
    each = functools.partial(lax.fori_loop, 0, 7)

    loads[0].wait()

    def viscosity(x, carry):
        for y in range(7):
            speed = [fv7[i, x, y].astype(jnp.float32) for i in range(3)]
            cv[x, y, 0:7, :] = 0.5 + 0.5 * (
                speed[0] * speed[0] + speed[1] * speed[1] + speed[2] * speed[2]
            )
            cv[x, y, 7:8, :] = zero_row
        return carry

    each(viscosity, 0)
    loads[3].wait()
    nwa = zc[NZ * 8 + 1]

    def coefficients(x, carry):
        wx, nwx = by_index(x, QW), by_index(x, NW)
        for y in range(7):
            base = cv[x, y] * nwa
            kx[x, y] = base * (wx * float(NW[y]))
            ky[x, y] = base * (nwx * float(QW[y]))
        return carry

    each(coefficients, 0)

    def remote(src, dst, send, recv, device):
        return pltpu.make_async_remote_copy(
            src_ref=src,
            dst_ref=dst,
            send_sem=send,
            recv_sem=recv,
            device_id=device,
            device_id_type=MESH,
        )

    setup_copies = [
        remote(kx.at[0], kx.at[7], set_send.at[0], set_recv.at[0], prev_x),
        remote(ky.at[:, 0], ky.at[:, 7], set_send.at[1], set_recv.at[1], prev_y),
        remote(bx.at[7], rb.at[0], set_send.at[2], set_recv.at[2], next_x),
        remote(by.at[:, 7], rb.at[1], set_send.at[3], set_recv.at[3], next_y),
    ]
    vecs = (v0, v1, v2, v3)

    def face_copies(r, c):
        extra = 2 if r == 0 else 1
        v = vecs[r]
        ends = (
            (v.at[c, 0], rv.at[r, c, 0], prev_x),
            (v.at[c, :, 0], rv.at[r, c, 1], prev_y),
            (s_out.at[r, c, 0, 0:extra], rs.at[r, c, 0, 0:extra], next_x),
            (s_out.at[r, c, 1, 0:extra], rs.at[r, c, 1, 0:extra], next_y),
        )
        return [
            remote(src, dst, send_sem.at[r, c, i], recv_sem.at[r, c, i], device)
            for i, (src, dst, device) in enumerate(ends)
        ]

    def start(copies):
        copies[0].start()
        pl.when(not_first)(copies[1].start)
        copies[2].start()
        pl.when(not_last)(copies[3].start)

    def wait_recv(copies):
        copies[0].wait_recv()
        pl.when(not_last)(copies[1].wait_recv)
        copies[2].wait_recv()
        pl.when(not_first)(copies[3].wait_recv)

    def wait_send(copies):
        copies[0].wait_send()
        pl.when(not_first)(copies[1].wait_send)
        copies[2].wait_send()
        pl.when(not_last)(copies[3].wait_send)

    pl.semaphore_wait(barrier, sum(GROUPS))
    setup_copies[0].start()
    pl.when(not_first)(setup_copies[1].start)

    def last_rows(i, carry):
        along_x = [kx[m, i] for m in range(7)]
        for k in range(8):
            bx[k, i] = total(float(DM[m, k] * DM[m, 7]) * along_x[m] for m in range(7))
        along_y = [ky[i, m] for m in range(7)]
        for k in range(8):
            by[i, k] = total(float(DM[m, k] * DM[m, 7]) * along_y[m] for m in range(7))
        return carry

    each(last_rows, 0)
    setup_copies[2].start()
    pl.when(not_last)(setup_copies[3].start)

    loads[1].wait()
    loads[2].wait()

    def spread_inputs(x, carry):
        nwx = by_index(x, NW)
        for c in range(3):
            for y in range(7):
                v0[c, x, y, 0:7, :] = x7[c, x, y]
                v0[c, x, y, 7:8, :] = zero_row
                fm[c, x, y, 0:7, :] = f7[c, x, y] * (nwa[0:7] * (nwx * float(NW[y])))
                fm[c, x, y, 7:8, :] = zero_row
        return carry

    each(spread_inputs, 0)

    for c in range(3):

        def first_sums(i, carry, c=c):
            v = [v0[c, k, i] for k in range(7)]
            s_out[0, c, 0, 0, i] = total(bx[k, i] * v[k] for k in range(7))
            s_out[0, c, 0, 1, i] = total(float(DM[7, k]) * v[k] for k in range(7))
            v = [v0[c, i, k] for k in range(7)]
            s_out[0, c, 1, 0, i] = total(by[i, k] * v[k] for k in range(7))
            s_out[0, c, 1, 1, i] = total(float(DM[7, k]) * v[k] for k in range(7))
            return carry

        each(first_sums, 0)
        start(face_copies(0, c))

    wz = zc[NZ * 8]

    def z_setup(x, carry):
        nwx = by_index(x, NW)
        for y in range(7):
            kz = close_rows(cv[x, y], last_row) * (wz * (nwx * float(NW[y])))
            turns = [turned(kz, t) for t in range(8)]
            for s in range(NZ):
                value = total(zc[s * 8 + t] * turns[t] for t in range(8))
                if s == 0:
                    value = value + nwa * (nwx * float(HELMHOLTZ * NW[y]))
                zd[x, y, s] = value
        return carry

    each(z_setup, 0)

    loads[4].wait()
    setup_copies[0].wait_recv()
    pl.when(not_last)(setup_copies[1].wait_recv)
    setup_copies[2].wait_recv()
    pl.when(not_first)(setup_copies[3].wait_recv)
    setup_copies[2].wait_send()
    pl.when(not_last)(setup_copies[3].wait_send)
    inner_y = jnp.where(not_first, D77 * D77, 0.0)

    def first_layers(i, carry):
        zd[0, i, 0] = zd[0, i, 0] + (rb[0, i] + (D77 * D77) * kx[0, i])
        zd[i, 0, 0] = zd[i, 0, 0] + (rb[1, i] + inner_y * ky[i, 0])
        return carry

    each(first_layers, 0)

    def x_diagonal(y, carry):
        kappa = [kx[m, y] for m in range(8)]
        for k in range(7):
            dg[k, y] = total(float(DM[m, k] ** 2) * kappa[m] for m in range(8))
            bx[k, y] = bx[k, y] + float(DM[7, k] * D77) * kappa[7]
        return carry

    each(x_diagonal, 0)

    def y_diagonal(x, carry):
        kappa = [ky[x, m] for m in range(8)]
        for k in range(7):
            value = total(float(DM[m, k] ** 2) * kappa[m] for m in range(8))
            by[x, k] = by[x, k] + float(DM[7, k] * D77) * kappa[7]
            value = value + dg[x, k] + fold_rows(zd[x, k, 0], first_row)
            value = jnp.where(last_row, 1.0, value)
            dg[x, k] = value
            mdi[x, k, 0:7, :] = m7[x, k].astype(jnp.float32) / value[0:7]
            mdi[x, k, 7:8, :] = zero_row
        return carry

    each(y_diagonal, 0)

    def local_apply(r):
        v_ref = vecs[r]
        for c in range(3):

            def x_lines(y, carry, c=c):
                out = line_apply([v_ref[c, k, y] for k in range(7)], [kx[m, y] for m in range(8)])
                for k in range(7):
                    acc[c, k, y] = out[k]
                return carry

            each(x_lines, 0)

            def yz_lines(x, carry, c=c):
                v = [v_ref[c, x, k] for k in range(7)]
                out = line_apply(v, [ky[x, m] for m in range(8)])
                for k in range(7):
                    z_part = z_apply(
                        close_rows(v[k], last_row), [zd[x, k, s] for s in range(NZ)], first_row
                    )
                    acc[c, x, k] = acc[c, x, k] + out[k] + z_part
                return carry

            each(yz_lines, 0)

    zero_tile = jnp.zeros((8, 128), jnp.float32)
    moments = {}

    def finish(r, c):
        v_ref, u_ref = vecs[r], vecs[r + 1]
        for i in range(7):
            sum_x, sum_y = rs[r, c, 0, 0, i], rs[r, c, 1, 0, i]
            if r == 0:
                sum_x = sum_x + D77 * kx[0, i] * rs[r, c, 0, 1, i]
                sum_y = sum_y + D77 * ky[i, 0] * rs[r, c, 1, 1, i]
            acc[c, 0, i] = acc[c, 0, i] + sum_x
            acc[c, i, 0] = acc[c, i, 0] + sum_y

        def row(x, carry):
            sums, tally = carry
            sums, tally = list(sums), list(tally)
            end_y = rv[r, c, 1, x]
            sum_y = []
            for y in range(7):
                b_x, b_y = bx[x, y], by[x, y]
                t = acc[c, x, y] + b_x * rv[r, c, 0, y] + b_y * end_y
                if r == 0:
                    u = mdi[x, y] * (fm[c, x, y] - t)
                else:
                    v = v_ref[c, x, y]
                    u = v - mdi[x, y] * t
                u_ref[c, x, y] = u
                if r < 2:
                    sums[y] = sums[y] + b_x * u
                    sum_y.append(b_y * u)
                weighted = dg[x, y] * u
                if r:
                    tally[0] = tally[0] + v * weighted
                tally[1] = tally[1] + u * weighted
            if r < 2:
                s_out[r + 1, c, 1, 0, x] = total(sum_y)
            return tuple(sums), tuple(tally)

        sums, tally = each(row, ((zero_tile,) * (7 if r < 2 else 0), (zero_tile,) * 2))
        if r < 2:
            for y in range(7):
                s_out[r + 1, c, 0, 0, y] = sums[y]
        if r:
            moments[2 * r - 1, c] = tally[0]
        moments[2 * r, c] = tally[1]

    for r in range(3):
        local_apply(r)
        for c in range(3):
            wait_recv(face_copies(r, c))
            finish(r, c)
            if r < 2:
                start(face_copies(r + 1, c))

    halves = []
    for half in range(2):
        stack = zero_tile
        for j in range(8):
            index = half * 8 + j
            if index < 15:
                value = jnp.sum(moments[index // 3, index % 3], axis=0, keepdims=True)
                stack = jnp.where(rows == j, value, stack)
        value = jnp.sum(stack, axis=1, keepdims=True)
        halves.append(jnp.where(lanes == rows + 8 * half, value, 0.0))
    row_total = jnp.sum(halves[0] + halves[1], axis=0, keepdims=True)

    for phase in range(2):
        count = GROUPS[phase]
        row_out[phase] = row_total
        for slot, device in enumerate(partners[phase]):
            remote(
                row_out.at[phase],
                rows_in.at[phase, slot],
                row_send.at[phase],
                row_recv.at[phase],
                device,
            ).start()
        everything = rows_in.at[phase, pl.ds(0, count)]
        pltpu.make_async_copy(everything, everything, row_recv.at[phase]).wait()
        row_total = total([row_total] + [rows_in[phase, slot] for slot in range(count)])

    n = []
    for k in range(5):
        picked = jnp.where(lanes == rows + 3 * k, jnp.broadcast_to(row_total, (8, 128)), 0.0)
        n.append(jnp.broadcast_to(jnp.sum(picked, axis=1, keepdims=True), (8, 128)))
    alpha0 = n[0] / (n[0] - n[1])
    a = -n[1] / (n[0] - n[1])
    e1 = a * a * n[0] + 2.0 * a * alpha0 * n[1] + alpha0 * alpha0 * n[2]
    b = a + e1 / n[0]
    curvature = (
        b * b * (n[0] - n[1]) + 2.0 * b * alpha0 * (n[1] - n[2]) + alpha0 * alpha0 * (n[2] - n[3])
    )
    alpha1 = e1 / curvature
    a0 = a - alpha1 * b
    a1 = alpha0 - alpha1 * (alpha0 - b)
    a2 = alpha1 * alpha0
    e2 = (
        a0 * a0 * n[0]
        + 2.0 * a0 * a1 * n[1]
        + (a1 * a1 + 2.0 * a0 * a2) * n[2]
        + 2.0 * a1 * a2 * n[3]
        + a2 * a2 * n[4]
    )
    beta1 = e2 / e1
    coef[0] = alpha0 + alpha1 * b
    coef[1] = a2
    coef[2] = a0 + beta1 * b
    coef[3] = a1 + beta1 * alpha0
    coef[4] = a2

    setup_copies[0].wait_send()
    pl.when(not_first)(setup_copies[1].wait_send)
    for r in range(3):
        for c in range(3):
            wait_send(face_copies(r, c))
    for phase in range(2):
        everything = rows_in.at[phase, pl.ds(0, GROUPS[phase])]
        pltpu.make_async_copy(everything, everything, row_send.at[phase]).wait()


def body(forcing, initial_guess, forward_velocity, free_mask):
    field = (3, 7, 7, 8, 128)
    plane = (7, 7, 8, 128)
    f32 = jnp.float32
    hbm = pl.BlockSpec(memory_space=pl.ANY)
    vmem = pl.BlockSpec(memory_space=pltpu.VMEM)
    v1, v2, v3, coef = pl.pallas_call(
        main_kernel,
        out_shape=[jax.ShapeDtypeStruct(field, f32)] * 3
        + [jax.ShapeDtypeStruct((5, 8, 128), f32)],
        in_specs=[hbm] * 5,
        out_specs=[vmem] * 4,
        scratch_shapes=[
            pltpu.VMEM((3, 7, 7, 7, 128), f32),
            pltpu.VMEM((3, 7, 7, 7, 128), f32),
            pltpu.VMEM((3, 7, 7, 7, 128), jnp.bfloat16),
            pltpu.VMEM((7, 7, 7, 128), jnp.int32),
            pltpu.VMEM((NZ * 8 + 2, 8, 128), f32),
            pltpu.VMEM(field, f32),
            pltpu.VMEM(field, f32),
            pltpu.VMEM(plane, f32),
            pltpu.VMEM(field, f32),
            pltpu.VMEM((8, 7, 8, 128), f32),
            pltpu.VMEM((7, 8, 8, 128), f32),
            pltpu.VMEM((8, 7, 8, 128), f32),
            pltpu.VMEM((7, 8, 8, 128), f32),
            pltpu.VMEM((7, 7, NZ, 8, 128), f32),
            pltpu.VMEM(plane, f32),
            pltpu.VMEM(plane, f32),
            pltpu.VMEM((3, 3, 2, 2, 7, 8, 128), f32),
            pltpu.VMEM((3, 3, 2, 7, 8, 128), f32),
            pltpu.VMEM((3, 3, 2, 2, 7, 8, 128), f32),
            pltpu.VMEM((2, 7, 8, 128), f32),
            pltpu.VMEM((2, 1, 128), f32),
            pltpu.VMEM((2, 31, 1, 128), f32),
            pltpu.SemaphoreType.DMA((5,)),
            pltpu.SemaphoreType.DMA((3, 3, 4)),
            pltpu.SemaphoreType.DMA((3, 3, 4)),
            pltpu.SemaphoreType.DMA((4,)),
            pltpu.SemaphoreType.DMA((4,)),
            pltpu.SemaphoreType.DMA((2,)),
            pltpu.SemaphoreType.DMA((2,)),
        ],
        compiler_params=pltpu.CompilerParams(
            collective_id=0, has_side_effects=True, vmem_limit_bytes=32 << 20
        ),
    )(forcing, initial_guess, forward_velocity, free_mask, jnp.asarray(z_constants()))
    v1, v2, v3 = (v[..., :7, :] for v in (v1, v2, v3))
    coef = coef[:, :3, None, None, None, :]
    guess = initial_guess + coef[0] * v1 + coef[1] * v2
    direction = coef[2] * v1 + coef[3] * v2 + coef[4] * v3
    return guess, direction


def solution(mesh):
    placed = (
        P(None, "px", "py", None, None),
        P(None, "px", "py", None, None),
        P(None, "px", "py", None, None),
        P("px", "py", None, None),
    )
    return jax.shard_map(
        body,
        mesh=mesh,
        in_specs=placed,
        out_specs=(P(None, "px", "py", None, None), P(None, "px", "py", None, None)),
        check_vma=False,
    )
```

time: 395 us -> 47.2 us (0.12)
  blocking collectives: 311 us -> 0 us
  Pallas kernels: 0 us -> 40.1 us
  starting transfers between devices: 36.5 us -> 0 us
  matrix products: 14.2 us -> 0 us
  waiting for transfers between devices: 9.8 us -> 0 us
  other arithmetic: 8.82 us -> 1.24 us
  local copies, waits for them, and re-layouts: 11.6 us -> 4.94 us
    psum x4 -> x0, blocking collectives: 311 us -> none  [the longest x3 233 us: energy_sum(): lax.psum(jnp.sum(residual * precond, axis=(1, 2, 3, 4)), ('px', 'py'))]
    pallas_call x0 -> x1, Pallas kernels: none -> 40.1 us  [body(): pl.pallas_call(main_kernel, out_shape=[jax.ShapeDtypeStruct(field, f32)]...]
    ppermute x16 -> x0, starting transfers between devices: 36.5 us -> none  [the longest x8 19.6 us: passed_along(): return lax.ppermute(block, axis, route)]
    dot_general x21 -> x0, matrix products: 14.2 us -> none  [the longest x9 7.28 us: kernel(): jnp.einsum('mk,...k' + index_tail + '->...m' + index_tail, deriv_table, v...]
    ppermute x16 -> x0, waiting for transfers between devices: 9.8 us -> none  [the longest x8 5.23 us: passed_along(): return lax.ppermute(block, axis, route)]
  transfers between devices with their start and end apart: 16 -> 0, of which waited for: 8 -> 0; matrix products, arithmetic and copies ran while one was open for 5% -> 0% of each run, Pallas kernels for 0% -> 0%
where the time goes in v1:
time: 47.2 us; the launch traced here: 46.9 us
  Pallas kernels  40.1 us (85%)
  local copies, waits for them, and re-layouts  4.94 us (10%)
  other arithmetic  1.24 us (3%)
  between operations  0.66 us (1%)
    pallas_call x1, Pallas kernels, body(): pl.pallas_call(main_kernel, out_shape=[jax.ShapeDtypeStruct(field, f32)]...  40.1 us
    unnamed x10, local copies, waits for them, and re-layouts  4.94 us
    add x1, other arithmetic, body(): direction = coef[2] * v1 + coef[3] * v2 + coef[4] * v3  1.24 us

profile of v1, /device:TPU:1, one launch (start us, length us, event | category | flops | bytes accessed | tf_op | source)
XLA Modules:
  0.0 46.9 jit_solution(12374568423224227128)
XLA Ops:
  0.6 0.0 copy-start
  0.6 1.1 %copy-done = f32[3,7,7,7,128]{4,3,2,1,0:T(8,128)S(1)} copy-done((f32[3,7,7,7,128]{4,3,2,1,0:T(8,128)S(1)}, f32[3,7,7,7,128]{4,3,2,1,0:T(8,128)}, u32[]{:S(2)}) %copy-start) | copy-done | bytes 526872
  1.7 0.0 copy-start.1
  1.7 1.1 %copy-done.1 = f32[3,7,7,7,128]{4,3,2,1,0:T(8,128)S(1)} copy-done((f32[3,7,7,7,128]{4,3,2,1,0:T(8,128)S(1)}, f32[3,7,7,7,128]{4,3,2,1,0:T(8,128)}, u32[]{:S(2)}) %copy-start.1) | copy-done | bytes 526872
  2.8 0.0 copy-start.2
  2.8 1.0 %copy-done.2 = bf16[3,7,7,7,128]{4,3,2,1,0:T(8,128)(2,1)S(1)} copy-done((bf16[3,7,7,7,128]{4,3,2,1,0:T(8,128)(2,1)S(1)}, bf16[3,7,7,7,128]{4,3,2,1,0:T(8,128)(2,1)}, u32[]{:S(2)}) %copy-start.2) | copy-done | bytes 263448
  3.7 0.0 copy-start.3
  3.7 0.9 %copy-done.3 = s32[7,7,7,128]{3,2,1,0:T(8,128)S(1)} copy-done((s32[7,7,7,128]{3,2,1,0:T(8,128)S(1)}, s32[7,7,7,128]{3,2,1,0:T(8,128)}, u32[]{:S(2)}) %copy-start.3) | copy-done | bytes 175640
  4.7 0.0 copy-start.4
  4.7 0.9 %copy-done.4 = f32[42,8,128]{2,1,0:T(8,128)S(1)} copy-done((f32[42,8,128]{2,1,0:T(8,128)S(1)}, f32[42,8,128]{2,1,0:T(8,128)}, u32[]{:S(2)}) %copy-start.4) | copy-done | bytes 172056
  5.6 40.1 %shard_map.68 = (f32[3,7,7,8,128]{4,3,2,1,0:T(8,128)S(1)}, f32[3,7,7,8,128]{4,3,2,1,0:T(8,128)S(1)}, f32[3,7,7,8,128]{4,3,2,1,0:T(8,128)S(1)}, f32[5,8,128]{2,1,0:T(8,128)S(1)}) custom-call(f32[3,7,7,7,128]{4,3,2,1,0:T(8,128)S(1)} %copy-done.1, f32[3,7,7,7,128]{4,3,2,1,0:T(8,128)S(1)} %copy-done, bf16[3,7,7,7,128]{4,3,2,1,0:T(8,128)(2,1)S(1)} %copy-done.2, ...), custom_call_target="tpu_custom_call" | custom-call | tf_op jit(solution)/shard_map/pallas_call | solution.py:529
  45.7 1.2 %multiply_add_fusion = (f32[3,7,7,7,128]{4,3,2,1,0:T(8,128)}, f32[3,7,7,7,128]{4,3,2,1,0:T(8,128)}) fusion(f32[3,7,7,8,128]{4,3,2,1,0:T(8,128)S(1)} %get-tuple-element.9, f32[3,7,7,8,128]{4,3,2,1,0:T(8,128)S(1)} %get-tuple-element.8, f32[3,7,7,8,128]{4,3,2,1,0:T(8,128)S(1)} %get-tuple-element.7, f32[3,128]{1,0:T(4,128)S(1)} %get-tuple-element.13, ...), kind=kLoop, calls=%fused_computation | loop fusion | flops 1185408 | bytes 3168768 | tf_op jit(solution)/shard_map/add | solution.py:573
  (1 shorter events, 0.0 us)
Async XLA Ops:
  0.6 1.1 %copy-start = (f32[3,7,7,7,128]{4,3,2,1,0:T(8,128)S(1)}, f32[3,7,7,7,128]{4,3,2,1,0:T(8,128)}, u32[]{:S(2)}) copy-start(f32[3,7,7,7,128]{4,3,2,1,0:T(8,128)} %x_hbm.1) | copy-start | bytes 1580548
  1.7 1.1 %copy-start.1 = (f32[3,7,7,7,128]{4,3,2,1,0:T(8,128)S(1)}, f32[3,7,7,7,128]{4,3,2,1,0:T(8,128)}, u32[]{:S(2)}) copy-start(f32[3,7,7,7,128]{4,3,2,1,0:T(8,128)} %f_hbm.1) | copy-start | bytes 1580548
  2.8 1.0 %copy-start.2 = (bf16[3,7,7,7,128]{4,3,2,1,0:T(8,128)(2,1)S(1)}, bf16[3,7,7,7,128]{4,3,2,1,0:T(8,128)(2,1)}, u32[]{:S(2)}) copy-start(bf16[3,7,7,7,128]{4,3,2,1,0:T(8,128)(2,1)} %fv_hbm.1) | copy-start | bytes 790276
  3.7 0.9 %copy-start.3 = (s32[7,7,7,128]{3,2,1,0:T(8,128)S(1)}, s32[7,7,7,128]{3,2,1,0:T(8,128)}, u32[]{:S(2)}) copy-start(s32[7,7,7,128]{3,2,1,0:T(8,128)} %m_hbm.1) | copy-start | bytes 526852
  4.7 0.9 %copy-start.4 = (f32[42,8,128]{2,1,0:T(8,128)S(1)}, f32[42,8,128]{2,1,0:T(8,128)}, u32[]{:S(2)}) copy-start(f32[42,8,128]{2,1,0:T(8,128)} %constant.2.clone.z_hbm) | copy-start | bytes 516100

commit v2 on v1

--- a/solution.py
+++ b/solution.py
@@ -524,7 +524,7 @@
     field = (3, 7, 7, 8, 128)
     plane = (7, 7, 8, 128)
     f32 = jnp.float32
-    hbm = pl.BlockSpec(memory_space=pl.ANY)
+    hbm = pl.BlockSpec(memory_space=pltpu.HBM)
     vmem = pl.BlockSpec(memory_space=pltpu.VMEM)
     v1, v2, v3, coef = pl.pallas_call(
         main_kernel,
@@ -566,7 +566,7 @@
         compiler_params=pltpu.CompilerParams(
             collective_id=0, has_side_effects=True, vmem_limit_bytes=32 << 20
         ),
-    )(forcing, initial_guess, forward_velocity, free_mask, jnp.asarray(z_constants()))
+    )(*[pltpu.with_memory_space_constraint(q, pltpu.HBM) for q in (forcing, initial_guess, forward_velocity, free_mask, jnp.asarray(z_constants()))])
     v1, v2, v3 = (v[..., :7, :] for v in (v1, v2, v3))
     coef = coef[:, :3, None, None, None, :]
     guess = initial_guess + coef[0] * v1 + coef[1] * v2

time: 47.2 us -> 41.9 us (0.89)
  local copies, waits for them, and re-layouts: 4.94 us -> 0.01 us
    unnamed x10 -> x2, local copies, waits for them, and re-layouts: 4.94 us -> 0.01 us
where the time goes in v2:
time: 41.9 us; the launch traced here: 41.8 us
  Pallas kernels  39.9 us (95%)
  other arithmetic  1.23 us (3%)
  between operations  0.66 us (2%)
    pallas_call x1, Pallas kernels, body(): pl.pallas_call(main_kernel, out_shape=[jax.ShapeDtypeStruct(field, f32)]...  39.9 us
    add x1, other arithmetic, body(): direction = coef[2] * v1 + coef[3] * v2 + coef[4] * v3  1.23 us

profile of v2, /device:TPU:1, one launch (start us, length us, event | category | flops | bytes accessed | tf_op | source)
XLA Modules:
  0.0 41.8 jit_solution(2694674695754699804)
XLA Ops:
  0.6 0.0 copy-start
  0.6 39.9 %shard_map.68 = (f32[3,7,7,8,128]{4,3,2,1,0:T(8,128)S(1)}, f32[3,7,7,8,128]{4,3,2,1,0:T(8,128)S(1)}, f32[3,7,7,8,128]{4,3,2,1,0:T(8,128)S(1)}, f32[5,8,128]{2,1,0:T(8,128)S(1)}) custom-call(f32[3,7,7,7,128]{4,3,2,1,0:T(8,128)} %f_hbm.1, f32[3,7,7,7,128]{4,3,2,1,0:T(8,128)} %x_hbm.1, bf16[3,7,7,7,128]{4,3,2,1,0:T(8,128)(2,1)} %fv_hbm.1, ...), custom_call_target="tpu_custom_call" | custom-call | tf_op jit(solution)/shard_map/pallas_call | solution.py:529
  40.5 0.0 copy-done
  40.5 1.2 %multiply_add_fusion = (f32[3,7,7,7,128]{4,3,2,1,0:T(8,128)}, f32[3,7,7,7,128]{4,3,2,1,0:T(8,128)}) fusion(f32[3,7,7,8,128]{4,3,2,1,0:T(8,128)S(1)} %get-tuple-element.9, f32[3,7,7,8,128]{4,3,2,1,0:T(8,128)S(1)} %get-tuple-element.8, f32[3,7,7,8,128]{4,3,2,1,0:T(8,128)S(1)} %get-tuple-element.7, f32[3,128]{1,0:T(4,128)S(1)} %get-tuple-element.13, ...), kind=kLoop, calls=%fused_computation | loop fusion | flops 1185408 | bytes 3168768 | tf_op jit(solution)/shard_map/add | solution.py:573
  (1 shorter events, 0.0 us)
Async XLA Ops:
  0.6 39.9 %copy-start = (f32[3,7,7,7,128]{4,3,2,1,0:T(8,128)S(1)}, f32[3,7,7,7,128]{4,3,2,1,0:T(8,128)}, u32[]{:S(2)}) copy-start(f32[3,7,7,7,128]{4,3,2,1,0:T(8,128)} %x_hbm.1) | copy-start | bytes 1580548

commit v3 on v2

--- a/solution.py
+++ b/solution.py
@@ -84,6 +84,13 @@
     return jnp.where(i == 0, float(table[0]), inner)
 
 
+def by_table(i, table):
+    value = float(table[6])
+    for k in range(5, -1, -1):
+        value = jnp.where(i == k, float(table[k]), value)
+    return value
+
+
 def line_apply(v, kappa):
     p = [v[0]] + [v[j] + v[7 - j] for j in range(1, 4)]
     q = [v[0]] + [v[j] - v[7 - j] for j in range(1, 4)]
@@ -92,9 +99,13 @@
         even = total(EVEN[m][k] * p[k] for k in range(4))
         odd = total(ODD[m][k] * q[k] for k in range(4))
         first = kappa[m] * (odd + even)
-        last = kappa[7 - m] * (odd - even)
-        a.append(first - last)
-        b.append(first + last)
+        if 7 - m < len(kappa):
+            last = kappa[7 - m] * (odd - even)
+            a.append(first - last)
+            b.append(first + last)
+        else:
+            a.append(first)
+            b.append(first)
     out = [None] * 8
     for k in range(4):
         r = total(EVEN[m][k] * a[m] for m in range(4))
@@ -105,31 +116,21 @@
     return out[:7]
 
 
-def close_rows(tile, last_row):
-    moved = pltpu.roll(pltpu.roll(tile, 127, 1), 7, 0)
-    return jnp.where(last_row, moved, tile)
-
-
-def fold_rows(tile, first_row):
-    moved = pltpu.roll(pltpu.roll(tile, 1, 1), 1, 0)
-    return jnp.where(first_row, tile + moved, tile)
-
-
 def turned(tile, s):
     return pltpu.roll(tile, 8 - s, 0) if s else tile
 
 
-def z_apply(closed, diagonals, first_row):
+def z_apply(closed, diagonals):
     terms = [diagonals[0] * closed, diagonals[4] * turned(closed, 4)]
     for s in range(1, 4):
         terms.append(diagonals[s] * turned(closed, s))
         terms.append(pltpu.roll(diagonals[s] * closed, s, 0))
-    return fold_rows(total(terms), first_row)
+    return total(terms)
 
 
 def group(px, py, phase):
     x, y, c = px // 8, lax.rem(px // 2, 4), lax.rem(px, 2)
-    if phase == 0:
+    if phase == 1:
         offsets = [(0, 0, 0, d) for d in (4, 3, 5, 2, 6, 1, 7)]
     else:
         offsets = [
@@ -146,13 +147,13 @@
     return out
 
 
-GROUPS = (7, 31)
+GROUPS = (31, 7)
 
 
 def main_kernel(
     f_hbm, x_hbm, fv_hbm, m_hbm, z_hbm,
     v1, v2, v3, coef,
-    f7, x7, fv7, m7, zc, v0, fm, cv, acc, kx, ky, bx, by, zd, mdi, dg,
+    f7, x7, fv7, m7, zc, v0, fm, cv, closing, acc, kx, ky, bx, by, zd, mdi, dg,
     s_out, rv, rs, rb, row_out, rows_in,
     load_sem, send_sem, recv_sem, set_send, set_recv, row_send, row_recv,
 ):
@@ -174,7 +175,7 @@
 
     partners = [group(px, py, phase) for phase in (0, 1)]
     barrier = pltpu.get_barrier_semaphore()
-    for device in partners[1] + partners[0]:
+    for device in partners[0] + partners[1]:
         pl.semaphore_signal(barrier, inc=1, device_id=device, device_id_type=MESH)
 
     zero_row = jnp.zeros((1, 128), jnp.float32)
@@ -197,7 +198,7 @@
 
     rows = lax.broadcasted_iota(jnp.int32, (8, 128), 0)
     lanes = lax.broadcasted_iota(jnp.int32, (8, 128), 1)
-    first_row, last_row = rows == 0, rows == 7
+    last_row = rows == 7
     each = functools.partial(lax.fori_loop, 0, 7)
 
     loads[0].wait()
@@ -208,9 +209,9 @@
             cv[x, y, 0:7, :] = 0.5 + 0.5 * (
                 speed[0] * speed[0] + speed[1] * speed[1] + speed[2] * speed[2]
             )
-            cv[x, y, 7:8, :] = zero_row
-        return carry
-
+        return carry
+
+    cv[:, :, 7:8, :] = jnp.zeros((7, 7, 1, 128), jnp.float32)
     each(viscosity, 0)
     loads[3].wait()
     nwa = zc[NZ * 8 + 1]
@@ -323,10 +324,13 @@
 
     wz = zc[NZ * 8]
 
+    for x in range(7):
+        cv[x, :, 7, :] = pltpu.roll(cv[x, :, 0, :], 127, 1)
+
     def z_setup(x, carry):
         nwx = by_index(x, NW)
         for y in range(7):
-            kz = close_rows(cv[x, y], last_row) * (wz * (nwx * float(NW[y])))
+            kz = cv[x, y] * (wz * (nwx * float(NW[y])))
             turns = [turned(kz, t) for t in range(8)]
             for s in range(NZ):
                 value = total(zc[s * 8 + t] * turns[t] for t in range(8))
@@ -336,6 +340,40 @@
         return carry
 
     each(z_setup, 0)
+
+    def local_apply(r):
+        v_ref = vecs[r]
+        points = 8 if r else 7
+        for c in range(3):
+            for x in range(7):
+                closing[c, x] = pltpu.roll(v_ref[c, x, :, 0, :], 127, 1)
+        for c in range(3):
+
+            def x_lines(y, carry, c=c):
+                out = line_apply(
+                    [v_ref[c, k, y] for k in range(7)], [kx[m, y] for m in range(points)]
+                )
+                for k in range(7):
+                    acc[c, k, y] = out[k]
+                return carry
+
+            each(x_lines, 0)
+
+            def yz_lines(x, carry, c=c):
+                v = [v_ref[c, x, k] for k in range(7)]
+                out = line_apply(v, [ky[x, m] for m in range(points)])
+                for k in range(7):
+                    closed = jnp.where(last_row, closing[c, x, k : k + 1, :], v[k])
+                    z_part = z_apply(closed, [zd[x, k, s] for s in range(NZ)])
+                    acc[c, x, k] = acc[c, x, k] + out[k] + z_part
+                return carry
+
+            each(yz_lines, 0)
+        for c in range(3):
+            for x in range(7):
+                acc[c, x, :, 0, :] = acc[c, x, :, 0, :] + pltpu.roll(acc[c, x, :, 7, :], 1, 1)
+
+    local_apply(0)
 
     loads[4].wait()
     setup_copies[0].wait_recv()
@@ -347,8 +385,13 @@
     inner_y = jnp.where(not_first, D77 * D77, 0.0)
 
     def first_layers(i, carry):
-        zd[0, i, 0] = zd[0, i, 0] + (rb[0, i] + (D77 * D77) * kx[0, i])
-        zd[i, 0, 0] = zd[i, 0, 0] + (rb[1, i] + inner_y * ky[i, 0])
+        layer_x = rb[0, i] + (D77 * D77) * kx[0, i]
+        layer_y = rb[1, i] + inner_y * ky[i, 0]
+        zd[0, i, 0] = zd[0, i, 0] + layer_x
+        zd[i, 0, 0] = zd[i, 0, 0] + layer_y
+        for c in range(3):
+            acc[c, 0, i] = acc[c, 0, i] + layer_x * v0[c, 0, i]
+            acc[c, i, 0] = acc[c, i, 0] + layer_y * v0[c, i, 0]
         return carry
 
     each(first_layers, 0)
@@ -362,43 +405,21 @@
 
     each(x_diagonal, 0)
 
+    for x in range(7):
+        dg[x, :, 0, :] = dg[x, :, 0, :] + pltpu.roll(zd[x, :, 0, 7, :], 1, 1)
+
     def y_diagonal(x, carry):
         kappa = [ky[x, m] for m in range(8)]
         for k in range(7):
             value = total(float(DM[m, k] ** 2) * kappa[m] for m in range(8))
             by[x, k] = by[x, k] + float(DM[7, k] * D77) * kappa[7]
-            value = value + dg[x, k] + fold_rows(zd[x, k, 0], first_row)
-            value = jnp.where(last_row, 1.0, value)
-            dg[x, k] = value
+            value = value + dg[x, k] + zd[x, k, 0]
+            dg[x, k] = jnp.where(last_row, 0.0, value)
             mdi[x, k, 0:7, :] = m7[x, k].astype(jnp.float32) / value[0:7]
             mdi[x, k, 7:8, :] = zero_row
         return carry
 
     each(y_diagonal, 0)
-
-    def local_apply(r):
-        v_ref = vecs[r]
-        for c in range(3):
-
-            def x_lines(y, carry, c=c):
-                out = line_apply([v_ref[c, k, y] for k in range(7)], [kx[m, y] for m in range(8)])
-                for k in range(7):
-                    acc[c, k, y] = out[k]
-                return carry
-
-            each(x_lines, 0)
-
-            def yz_lines(x, carry, c=c):
-                v = [v_ref[c, x, k] for k in range(7)]
-                out = line_apply(v, [ky[x, m] for m in range(8)])
-                for k in range(7):
-                    z_part = z_apply(
-                        close_rows(v[k], last_row), [zd[x, k, s] for s in range(NZ)], first_row
-                    )
-                    acc[c, x, k] = acc[c, x, k] + out[k] + z_part
-                return carry
-
-            each(yz_lines, 0)
 
     zero_tile = jnp.zeros((8, 128), jnp.float32)
     moments = {}
@@ -418,10 +439,14 @@
             sums, tally = list(sums), list(tally)
             end_y = rv[r, c, 1, x]
             sum_y = []
+            if r == 0:
+                at_end = by_table(x, DM[7])
+                last_y = ky[x, 7] * s_out[0, c, 1, 1, x]
             for y in range(7):
                 b_x, b_y = bx[x, y], by[x, y]
                 t = acc[c, x, y] + b_x * rv[r, c, 0, y] + b_y * end_y
                 if r == 0:
+                    t = t + at_end * (kx[7, y] * s_out[0, c, 0, 1, y]) + float(DM[7, y]) * last_y
                     u = mdi[x, y] * (fm[c, x, y] - t)
                 else:
                     v = v_ref[c, x, y]
@@ -447,7 +472,8 @@
         moments[2 * r, c] = tally[1]
 
     for r in range(3):
-        local_apply(r)
+        if r:
+            local_apply(r)
         for c in range(3):
             wait_recv(face_copies(r, c))
             finish(r, c)
@@ -541,6 +567,7 @@
             pltpu.VMEM(field, f32),
             pltpu.VMEM(field, f32),
             pltpu.VMEM(plane, f32),
+            pltpu.VMEM((3, 7, 7, 128), f32),
             pltpu.VMEM(field, f32),
             pltpu.VMEM((8, 7, 8, 128), f32),
             pltpu.VMEM((7, 8, 8, 128), f32),

time: 41.9 us -> 36.6 us (0.87)
  Pallas kernels: 39.9 us -> 34.6 us
    pallas_call x1, Pallas kernels: 39.9 us -> 34.6 us  [body(): pl.pallas_call(main_kernel, out_shape=[jax.ShapeDtypeStruct(field, f32)]...]
where the time goes in v3:
time: 36.6 us; the launch traced here: 36.5 us
  Pallas kernels  34.6 us (95%)
  other arithmetic  1.23 us (3%)
  between operations  0.66 us (2%)
    pallas_call x1, Pallas kernels, body(): pl.pallas_call(main_kernel, out_shape=[jax.ShapeDtypeStruct(field, f32)]...  34.6 us
    add x1, other arithmetic, body(): direction = coef[2] * v1 + coef[3] * v2 + coef[4] * v3  1.23 us

profile of v3, /device:TPU:1, one launch (start us, length us, event | category | flops | bytes accessed | tf_op | source)
XLA Modules:
  0.0 36.5 jit_solution(2815133794369800548)
XLA Ops:
  0.6 0.0 copy-start
  0.6 34.6 %shard_map.68 = (f32[3,7,7,8,128]{4,3,2,1,0:T(8,128)S(1)}, f32[3,7,7,8,128]{4,3,2,1,0:T(8,128)S(1)}, f32[3,7,7,8,128]{4,3,2,1,0:T(8,128)S(1)}, f32[5,8,128]{2,1,0:T(8,128)S(1)}) custom-call(f32[3,7,7,7,128]{4,3,2,1,0:T(8,128)} %f_hbm.1, f32[3,7,7,7,128]{4,3,2,1,0:T(8,128)} %x_hbm.1, bf16[3,7,7,7,128]{4,3,2,1,0:T(8,128)(2,1)} %fv_hbm.1, ...), custom_call_target="tpu_custom_call" | custom-call | tf_op jit(solution)/shard_map/pallas_call | solution.py:555
  35.3 0.0 copy-done
  35.3 1.2 %multiply_add_fusion = (f32[3,7,7,7,128]{4,3,2,1,0:T(8,128)}, f32[3,7,7,7,128]{4,3,2,1,0:T(8,128)}) fusion(f32[3,7,7,8,128]{4,3,2,1,0:T(8,128)S(1)} %get-tuple-element.9, f32[3,7,7,8,128]{4,3,2,1,0:T(8,128)S(1)} %get-tuple-element.8, f32[3,7,7,8,128]{4,3,2,1,0:T(8,128)S(1)} %get-tuple-element.7, f32[3,128]{1,0:T(4,128)S(1)} %get-tuple-element.13, ...), kind=kLoop, calls=%fused_computation | loop fusion | flops 1185408 | bytes 3168768 | tf_op jit(solution)/shard_map/add | solution.py:600
  (1 shorter events, 0.0 us)
Async XLA Ops:
  0.6 34.7 %copy-start = (f32[3,7,7,7,128]{4,3,2,1,0:T(8,128)S(1)}, f32[3,7,7,7,128]{4,3,2,1,0:T(8,128)}, u32[]{:S(2)}) copy-start(f32[3,7,7,7,128]{4,3,2,1,0:T(8,128)} %x_hbm.1) | copy-start | bytes 1580548

commit v4 on v3

--- a/solution.py
+++ b/solution.py
@@ -128,26 +128,9 @@
     return total(terms)
 
 
-def group(px, py, phase):
-    x, y, c = px // 8, lax.rem(px // 2, 4), lax.rem(px, 2)
-    if phase == 1:
-        offsets = [(0, 0, 0, d) for d in (4, 3, 5, 2, 6, 1, 7)]
-    else:
-        offsets = [
-            (dx, dy, dc, 0)
-            for dx in (2, 1, 3, 0)
-            for dy in (2, 1, 3, 0)
-            for dc in (1, 0)
-            if dx or dy or dc
-        ]
-    out = []
-    for dx, dy, dc, dz in offsets:
-        nx, ny, nc = lax.rem(x + dx, 4), lax.rem(y + dy, 4), lax.rem(c + dc, 2)
-        out.append((nx * 8 + ny * 2 + nc, lax.rem(py + dz, 8)))
-    return out
-
-
-GROUPS = (31, 7)
+CHIPS = 128
+Z_ORDER = (4, 3, 5, 2, 6, 1, 7, 0)
+GREETINGS = (("z", 1), ("z", 2), ("x", 1), ("x", 1), ("y", 1), ("y", 1))
 
 
 def main_kernel(
@@ -155,7 +138,7 @@
     v1, v2, v3, coef,
     f7, x7, fv7, m7, zc, v0, fm, cv, closing, acc, kx, ky, bx, by, zd, mdi, dg,
     s_out, rv, rs, rb, row_out, rows_in,
-    load_sem, send_sem, recv_sem, set_send, set_recv, row_send, row_recv,
+    load_sem, send_sem, recv_sem, set_send, set_recv, row_send, row_recv, greet_sem,
 ):
     px = lax.axis_index("px")
     py = lax.axis_index("py")
@@ -173,10 +156,30 @@
     for load in loads:
         load.start()
 
-    partners = [group(px, py, phase) for phase in (0, 1)]
+    at = {"x": px // 8, "y": lax.rem(px // 2, 4), "z": py}
+    core = lax.rem(px, 2)
+    other_core = (px + 1 - 2 * core, py)
+
+    def chip(x=0, y=0, z=0):
+        nx, ny, nz = lax.rem(at["x"] + x, 4), lax.rem(at["y"] + y, 4), lax.rem(at["z"] + z, 8)
+        return (nx * 8 + ny * 2 + core, nz)
+
+    def around(axis, distance):
+        return chip(**{axis: distance}), chip(**{axis: (8 if axis == "z" else 4) - distance})
+
     barrier = pltpu.get_barrier_semaphore()
-    for device in partners[0] + partners[1]:
+    greeted = (*around("y", 1), *around("x", 1), *around("z", 1), prev_x, next_x)
+    for device in greeted:
         pl.semaphore_signal(barrier, inc=1, device_id=device, device_id_type=MESH)
+
+    def greet(step):
+        if step:
+            pl.semaphore_wait(greet_sem.at[step - 1], 2)
+        if step < len(GREETINGS):
+            for device in around(*GREETINGS[step]):
+                pl.semaphore_signal(
+                    greet_sem.at[step], inc=1, device_id=device, device_id_type=MESH
+                )
 
     zero_row = jnp.zeros((1, 128), jnp.float32)
     zero_face = jnp.zeros((7, 8, 128), jnp.float32)
@@ -276,9 +279,10 @@
         copies[2].wait_send()
         pl.when(not_last)(copies[3].wait_send)
 
-    pl.semaphore_wait(barrier, sum(GROUPS))
+    pl.semaphore_wait(barrier, len(greeted))
     setup_copies[0].start()
     pl.when(not_first)(setup_copies[1].start)
+    greet(0)
 
     def last_rows(i, carry):
         along_x = [kx[m, i] for m in range(7)]
@@ -321,6 +325,8 @@
 
         each(first_sums, 0)
         start(face_copies(0, c))
+
+    greet(1)
 
     wz = zc[NZ * 8]
 
@@ -340,6 +346,7 @@
         return carry
 
     each(z_setup, 0)
+    greet(2)
 
     def local_apply(r):
         v_ref = vecs[r]
@@ -374,6 +381,7 @@
                 acc[c, x, :, 0, :] = acc[c, x, :, 0, :] + pltpu.roll(acc[c, x, :, 7, :], 1, 1)
 
     local_apply(0)
+    greet(3)
 
     loads[4].wait()
     setup_copies[0].wait_recv()
@@ -474,11 +482,14 @@
     for r in range(3):
         if r:
             local_apply(r)
+            greet(4 + r)
         for c in range(3):
             wait_recv(face_copies(r, c))
             finish(r, c)
             if r < 2:
                 start(face_copies(r + 1, c))
+        if r == 0:
+            greet(4)
 
     halves = []
     for half in range(2):
@@ -492,20 +503,28 @@
         halves.append(jnp.where(lanes == rows + 8 * half, value, 0.0))
     row_total = jnp.sum(halves[0] + halves[1], axis=0, keepdims=True)
 
-    for phase in range(2):
-        count = GROUPS[phase]
-        row_out[phase] = row_total
-        for slot, device in enumerate(partners[phase]):
+    row_out[0] = row_total
+    pair = remote(row_out.at[0], rows_in.at[CHIPS - 1], row_send.at[0], row_recv.at[0], other_core)
+    pair.start()
+    pair.wait_recv()
+    row_total = row_total + rows_in[CHIPS - 1]
+    row_out[1] = row_total
+    for place, dz in enumerate(Z_ORDER):
+
+        def send(i, carry, place=place, dz=dz):
             remote(
-                row_out.at[phase],
-                rows_in.at[phase, slot],
-                row_send.at[phase],
-                row_recv.at[phase],
-                device,
+                row_out.at[1],
+                rows_in.at[16 * place + i],
+                row_send.at[1],
+                row_recv.at[1],
+                chip(3 - i // 4, 3 - lax.rem(i, 4), dz),
             ).start()
-        everything = rows_in.at[phase, pl.ds(0, count)]
-        pltpu.make_async_copy(everything, everything, row_recv.at[phase]).wait()
-        row_total = total([row_total] + [rows_in[phase, slot] for slot in range(count)])
+            return carry
+
+        lax.fori_loop(0, 16 if dz else 15, send, 0)
+    everything = rows_in.at[pl.ds(0, CHIPS - 1)]
+    pltpu.make_async_copy(everything, everything, row_recv.at[1]).wait()
+    row_total = total([row_total] + [rows_in[slot] for slot in range(CHIPS - 1)])
 
     n = []
     for k in range(5):
@@ -541,9 +560,8 @@
     for r in range(3):
         for c in range(3):
             wait_send(face_copies(r, c))
-    for phase in range(2):
-        everything = rows_in.at[phase, pl.ds(0, GROUPS[phase])]
-        pltpu.make_async_copy(everything, everything, row_send.at[phase]).wait()
+    pair.wait_send()
+    pltpu.make_async_copy(everything, everything, row_send.at[1]).wait()
 
 
 def body(forcing, initial_guess, forward_velocity, free_mask):
@@ -581,7 +599,7 @@
             pltpu.VMEM((3, 3, 2, 2, 7, 8, 128), f32),
             pltpu.VMEM((2, 7, 8, 128), f32),
             pltpu.VMEM((2, 1, 128), f32),
-            pltpu.VMEM((2, 31, 1, 128), f32),
+            pltpu.VMEM((CHIPS, 1, 128), f32),
             pltpu.SemaphoreType.DMA((5,)),
             pltpu.SemaphoreType.DMA((3, 3, 4)),
             pltpu.SemaphoreType.DMA((3, 3, 4)),
@@ -589,6 +607,7 @@
             pltpu.SemaphoreType.DMA((4,)),
             pltpu.SemaphoreType.DMA((2,)),
             pltpu.SemaphoreType.DMA((2,)),
+            pltpu.SemaphoreType.REGULAR((len(GREETINGS),)),
         ],
         compiler_params=pltpu.CompilerParams(
             collective_id=0, has_side_effects=True, vmem_limit_bytes=32 << 20

time: 36.6 us -> 34.4 us (0.940)
  Pallas kernels: 34.6 us -> 32.4 us
    pallas_call x1, Pallas kernels: 34.6 us -> 32.4 us  [body(): pl.pallas_call(main_kernel, out_shape=[jax.ShapeDtypeStruct(field, f32)]...]
where the time goes in v4:
time: 34.4 us; the launch traced here: 34.3 us
  Pallas kernels  32.4 us (94%)
  other arithmetic  1.23 us (4%)
  between operations  0.66 us (2%)
    pallas_call x1, Pallas kernels, body(): pl.pallas_call(main_kernel, out_shape=[jax.ShapeDtypeStruct(field, f32)]...  32.4 us
    add x1, other arithmetic, body(): direction = coef[2] * v1 + coef[3] * v2 + coef[4] * v3  1.23 us

profile of v4, /device:TPU:1, one launch (start us, length us, event | category | flops | bytes accessed | tf_op | source)
XLA Modules:
  0.0 34.3 jit_solution(7064106115461344148)
XLA Ops:
  0.6 0.0 copy-start
  0.6 32.4 %shard_map.68 = (f32[3,7,7,8,128]{4,3,2,1,0:T(8,128)S(1)}, f32[3,7,7,8,128]{4,3,2,1,0:T(8,128)S(1)}, f32[3,7,7,8,128]{4,3,2,1,0:T(8,128)S(1)}, f32[5,8,128]{2,1,0:T(8,128)S(1)}) custom-call(f32[3,7,7,7,128]{4,3,2,1,0:T(8,128)} %f_hbm.1, f32[3,7,7,7,128]{4,3,2,1,0:T(8,128)} %x_hbm.1, bf16[3,7,7,7,128]{4,3,2,1,0:T(8,128)(2,1)} %fv_hbm.1, ...), custom_call_target="tpu_custom_call" | custom-call | tf_op jit(solution)/shard_map/pallas_call | solution.py:573
  33.1 0.0 copy-done
  33.1 1.2 %multiply_add_fusion = (f32[3,7,7,7,128]{4,3,2,1,0:T(8,128)}, f32[3,7,7,7,128]{4,3,2,1,0:T(8,128)}) fusion(f32[3,7,7,8,128]{4,3,2,1,0:T(8,128)S(1)} %get-tuple-element.9, f32[3,7,7,8,128]{4,3,2,1,0:T(8,128)S(1)} %get-tuple-element.8, f32[3,7,7,8,128]{4,3,2,1,0:T(8,128)S(1)} %get-tuple-element.7, f32[3,128]{1,0:T(4,128)S(1)} %get-tuple-element.13, ...), kind=kLoop, calls=%fused_computation | loop fusion | flops 1185408 | bytes 3168768 | tf_op jit(solution)/shard_map/add | solution.py:619
  (1 shorter events, 0.0 us)
Async XLA Ops:
  0.6 32.4 %copy-start = (f32[3,7,7,7,128]{4,3,2,1,0:T(8,128)S(1)}, f32[3,7,7,7,128]{4,3,2,1,0:T(8,128)}, u32[]{:S(2)}) copy-start(f32[3,7,7,7,128]{4,3,2,1,0:T(8,128)} %x_hbm.1) | copy-start | bytes 1580548

commit v5 on v4

--- a/solution.py
+++ b/solution.py
@@ -203,6 +203,7 @@
     lanes = lax.broadcasted_iota(jnp.int32, (8, 128), 1)
     last_row = rows == 7
     each = functools.partial(lax.fori_loop, 0, 7)
+    whole = functools.partial(lax.fori_loop, 0, 7, unroll=True)
 
     loads[0].wait()
 
@@ -215,7 +216,7 @@
         return carry
 
     cv[:, :, 7:8, :] = jnp.zeros((7, 7, 1, 128), jnp.float32)
-    each(viscosity, 0)
+    whole(viscosity, 0)
     loads[3].wait()
     nwa = zc[NZ * 8 + 1]
 
@@ -227,7 +228,7 @@
             ky[x, y] = base * (nwx * float(QW[y]))
         return carry
 
-    each(coefficients, 0)
+    whole(coefficients, 0)
 
     def remote(src, dst, send, recv, device):
         return pltpu.make_async_remote_copy(
@@ -279,11 +280,6 @@
         copies[2].wait_send()
         pl.when(not_last)(copies[3].wait_send)
 
-    pl.semaphore_wait(barrier, len(greeted))
-    setup_copies[0].start()
-    pl.when(not_first)(setup_copies[1].start)
-    greet(0)
-
     def last_rows(i, carry):
         along_x = [kx[m, i] for m in range(7)]
         for k in range(8):
@@ -293,24 +289,18 @@
             by[i, k] = total(float(DM[m, k] * DM[m, 7]) * along_y[m] for m in range(7))
         return carry
 
-    each(last_rows, 0)
-    setup_copies[2].start()
-    pl.when(not_last)(setup_copies[3].start)
+    whole(last_rows, 0)
 
     loads[1].wait()
-    loads[2].wait()
-
-    def spread_inputs(x, carry):
-        nwx = by_index(x, NW)
+
+    def spread_guess(x, carry):
         for c in range(3):
             for y in range(7):
                 v0[c, x, y, 0:7, :] = x7[c, x, y]
                 v0[c, x, y, 7:8, :] = zero_row
-                fm[c, x, y, 0:7, :] = f7[c, x, y] * (nwa[0:7] * (nwx * float(NW[y])))
-                fm[c, x, y, 7:8, :] = zero_row
-        return carry
-
-    each(spread_inputs, 0)
+        return carry
+
+    whole(spread_guess, 0)
 
     for c in range(3):
 
@@ -323,10 +313,28 @@
             s_out[0, c, 1, 1, i] = total(float(DM[7, k]) * v[k] for k in range(7))
             return carry
 
-        each(first_sums, 0)
+        whole(first_sums, 0)
+
+    pl.semaphore_wait(barrier, len(greeted))
+    greet(0)
+    setup_copies[0].start()
+    pl.when(not_first)(setup_copies[1].start)
+    setup_copies[2].start()
+    pl.when(not_last)(setup_copies[3].start)
+    for c in range(3):
         start(face_copies(0, c))
 
-    greet(1)
+    loads[2].wait()
+
+    def spread_forcing(x, carry):
+        nwx = by_index(x, NW)
+        for c in range(3):
+            for y in range(7):
+                fm[c, x, y, 0:7, :] = f7[c, x, y] * (nwa[0:7] * (nwx * float(NW[y])))
+                fm[c, x, y, 7:8, :] = zero_row
+        return carry
+
+    each(spread_forcing, 0)
 
     wz = zc[NZ * 8]
 
@@ -346,7 +354,7 @@
         return carry
 
     each(z_setup, 0)
-    greet(2)
+    greet(1)
 
     def local_apply(r):
         v_ref = vecs[r]
@@ -381,7 +389,7 @@
                 acc[c, x, :, 0, :] = acc[c, x, :, 0, :] + pltpu.roll(acc[c, x, :, 7, :], 1, 1)
 
     local_apply(0)
-    greet(3)
+    greet(2)
 
     loads[4].wait()
     setup_copies[0].wait_recv()
@@ -428,6 +436,7 @@
         return carry
 
     each(y_diagonal, 0)
+    greet(3)
 
     zero_tile = jnp.zeros((8, 128), jnp.float32)
     moments = {}
@@ -471,7 +480,7 @@
                 s_out[r + 1, c, 1, 0, x] = total(sum_y)
             return tuple(sums), tuple(tally)
 
-        sums, tally = each(row, ((zero_tile,) * (7 if r < 2 else 0), (zero_tile,) * 2))
+        sums, tally = whole(row, ((zero_tile,) * (7 if r < 2 else 0), (zero_tile,) * 2))
         if r < 2:
             for y in range(7):
                 s_out[r + 1, c, 0, 0, y] = sums[y]
@@ -482,7 +491,8 @@
     for r in range(3):
         if r:
             local_apply(r)
-            greet(4 + r)
+            if r == 1:
+                greet(5)
         for c in range(3):
             wait_recv(face_copies(r, c))
             finish(r, c)
@@ -490,6 +500,8 @@
                 start(face_copies(r + 1, c))
         if r == 0:
             greet(4)
+        if r == 1:
+            greet(6)
 
     halves = []
     for half in range(2):

time: 34.4 us -> 33.8 us (0.983)
  Pallas kernels: 32.4 us -> 31.8 us
    pallas_call x1, Pallas kernels: 32.4 us -> 31.8 us  [body(): pl.pallas_call(main_kernel, out_shape=[jax.ShapeDtypeStruct(field, f32)]...]
where the time goes in v5:
time: 33.8 us; the launch traced here: 33.7 us
  Pallas kernels  31.8 us (94%)
  other arithmetic  1.23 us (4%)
  between operations  0.66 us (2%)
    pallas_call x1, Pallas kernels, body(): pl.pallas_call(main_kernel, out_shape=[jax.ShapeDtypeStruct(field, f32)]...  31.8 us
    add x1, other arithmetic, body(): direction = coef[2] * v1 + coef[3] * v2 + coef[4] * v3  1.23 us

profile of v5, /device:TPU:1, one launch (start us, length us, event | category | flops | bytes accessed | tf_op | source)
XLA Modules:
  0.0 33.7 jit_solution(10443285593892434830)
XLA Ops:
  0.6 0.0 copy-start
  0.6 31.8 %shard_map.68 = (f32[3,7,7,8,128]{4,3,2,1,0:T(8,128)S(1)}, f32[3,7,7,8,128]{4,3,2,1,0:T(8,128)S(1)}, f32[3,7,7,8,128]{4,3,2,1,0:T(8,128)S(1)}, f32[5,8,128]{2,1,0:T(8,128)S(1)}) custom-call(f32[3,7,7,7,128]{4,3,2,1,0:T(8,128)} %f_hbm.1, f32[3,7,7,7,128]{4,3,2,1,0:T(8,128)} %x_hbm.1, bf16[3,7,7,7,128]{4,3,2,1,0:T(8,128)(2,1)} %fv_hbm.1, ...), custom_call_target="tpu_custom_call" | custom-call | tf_op jit(solution)/shard_map/pallas_call | solution.py:585
  32.4 0.0 copy-done
  32.4 1.2 %multiply_add_fusion = (f32[3,7,7,7,128]{4,3,2,1,0:T(8,128)}, f32[3,7,7,7,128]{4,3,2,1,0:T(8,128)}) fusion(f32[3,7,7,8,128]{4,3,2,1,0:T(8,128)S(1)} %get-tuple-element.9, f32[3,7,7,8,128]{4,3,2,1,0:T(8,128)S(1)} %get-tuple-element.8, f32[3,7,7,8,128]{4,3,2,1,0:T(8,128)S(1)} %get-tuple-element.7, f32[3,128]{1,0:T(4,128)S(1)} %get-tuple-element.13, ...), kind=kLoop, calls=%fused_computation | loop fusion | flops 1185408 | bytes 3168768 | tf_op jit(solution)/shard_map/add | solution.py:631
  (1 shorter events, 0.0 us)
Async XLA Ops:
  0.6 31.8 %copy-start = (f32[3,7,7,7,128]{4,3,2,1,0:T(8,128)S(1)}, f32[3,7,7,7,128]{4,3,2,1,0:T(8,128)}, u32[]{:S(2)}) copy-start(f32[3,7,7,7,128]{4,3,2,1,0:T(8,128)} %x_hbm.1) | copy-start | bytes 1580548

commit v6 on v5

--- a/solution.py
+++ b/solution.py
@@ -263,10 +263,10 @@
         ]
 
     def start(copies):
+        pl.when(not_last)(copies[3].start)
+        copies[2].start()
+        pl.when(not_first)(copies[1].start)
         copies[0].start()
-        pl.when(not_first)(copies[1].start)
-        copies[2].start()
-        pl.when(not_last)(copies[3].start)
 
     def wait_recv(copies):
         copies[0].wait_recv()
@@ -533,7 +533,7 @@
             ).start()
             return carry
 
-        lax.fori_loop(0, 16 if dz else 15, send, 0)
+        lax.fori_loop(0, 16 if dz else 15, send, 0, unroll=4 if dz else 5)
     everything = rows_in.at[pl.ds(0, CHIPS - 1)]
     pltpu.make_async_copy(everything, everything, row_recv.at[1]).wait()
     row_total = total([row_total] + [rows_in[slot] for slot in range(CHIPS - 1)])

time: 33.8 us -> 33.7 us (level)
  no operation moved by 1% of the time
where the time goes in v6:
time: 33.7 us; the launch traced here: 33.6 us
  Pallas kernels  31.7 us (94%)
  other arithmetic  1.23 us (4%)
  between operations  0.66 us (2%)
    pallas_call x1, Pallas kernels, body(): pl.pallas_call(main_kernel, out_shape=[jax.ShapeDtypeStruct(field, f32)]...  31.7 us
    add x1, other arithmetic, body(): direction = coef[2] * v1 + coef[3] * v2 + coef[4] * v3  1.23 us

profile of v6, /device:TPU:1, one launch (start us, length us, event | category | flops | bytes accessed | tf_op | source)
XLA Modules:
  0.0 33.6 jit_solution(12545652366300049976)
XLA Ops:
  0.6 0.0 copy-start
  0.6 31.7 %shard_map.68 = (f32[3,7,7,8,128]{4,3,2,1,0:T(8,128)S(1)}, f32[3,7,7,8,128]{4,3,2,1,0:T(8,128)S(1)}, f32[3,7,7,8,128]{4,3,2,1,0:T(8,128)S(1)}, f32[5,8,128]{2,1,0:T(8,128)S(1)}) custom-call(f32[3,7,7,7,128]{4,3,2,1,0:T(8,128)} %f_hbm.1, f32[3,7,7,7,128]{4,3,2,1,0:T(8,128)} %x_hbm.1, bf16[3,7,7,7,128]{4,3,2,1,0:T(8,128)(2,1)} %fv_hbm.1, ...), custom_call_target="tpu_custom_call" | custom-call | tf_op jit(solution)/shard_map/pallas_call | solution.py:585
  32.4 0.0 copy-done
  32.4 1.2 %multiply_add_fusion = (f32[3,7,7,7,128]{4,3,2,1,0:T(8,128)}, f32[3,7,7,7,128]{4,3,2,1,0:T(8,128)}) fusion(f32[3,7,7,8,128]{4,3,2,1,0:T(8,128)S(1)} %get-tuple-element.9, f32[3,7,7,8,128]{4,3,2,1,0:T(8,128)S(1)} %get-tuple-element.8, f32[3,7,7,8,128]{4,3,2,1,0:T(8,128)S(1)} %get-tuple-element.7, f32[3,128]{1,0:T(4,128)S(1)} %get-tuple-element.13, ...), kind=kLoop, calls=%fused_computation | loop fusion | flops 1185408 | bytes 3168768 | tf_op jit(solution)/shard_map/add | solution.py:631
  (1 shorter events, 0.0 us)
Async XLA Ops:
  0.6 31.8 %copy-start = (f32[3,7,7,7,128]{4,3,2,1,0:T(8,128)S(1)}, f32[3,7,7,7,128]{4,3,2,1,0:T(8,128)}, u32[]{:S(2)}) copy-start(f32[3,7,7,7,128]{4,3,2,1,0:T(8,128)} %x_hbm.1) | copy-start | bytes 1580548
